TPU v7x, 32 devices: a whole 2x2x4 slice. The times are simulated.
32 devices in a mesh: rows: 32 (over z, y, x, core), sub: 1.
Axes of the slice: x: 2, y: 2, z: 4, core: 2. Of those that a mesh axis runs over, the one named last changes fastest.
Arguments:
- embeddings: bfloat16 [16384, 1024], P('rows', 'sub'), may hold values from -40 to 40
- rotation: bfloat16 [1024, 1024], P(None, 'sub'), may hold values from -0.1875 to 0.1875
- codebooks: float32 [64, 16, 256], P('sub'), may hold values from -6 to 6
Outputs:
- new_codebooks: float32 [64, 16, 256], P('sub')
- new_rotation: float32 [1024, 1024], P('rows', 'sub')
All inputs are finite; a program needn't handle non-finite values.
Results may differ from a plain program's by a relative error of at most 0.006.
The roundings to bfloat16 on the way count: a program that leaves them out, or rounds other values in their place, can miss the bound.
Values may be sent and summed in bfloat16 or wider, within the bound.
A program may use at most 64 MiB of HBM per device.

v0:
```python
import functools

import jax
import jax.numpy as jnp
from jax import lax
from jax.experimental import pallas as pl
from jax.experimental.pallas import tpu as pltpu
from jax.sharding import PartitionSpec as P

SUB_DIM = 16
ITERS = 2
LOG2E = 1.4426950408889634
STAT_ROWS = 24

prior_weight = 8.0
quintic_one = 3.4445
quintic_three = -4.775
quintic_five = 2.0315
MESH = pl.DeviceIdType.MESH


def split_three(value):
    high = value.astype(jnp.bfloat16)
    rest = value - high.astype(jnp.float32)
    middle = rest.astype(jnp.bfloat16)
    low = (rest - middle.astype(jnp.float32)).astype(jnp.bfloat16)
    return high, middle, low


def pass_kernel(feat_ref, book_ref, stats_ref, *weights_refs):
    group, dim, rows = feat_ref.shape
    codes = book_ref.shape[2]
    chunk = 256 if rows % 256 == 0 else rows
    ones = jnp.ones((16, rows), jnp.bfloat16)
    row = lax.broadcasted_iota(jnp.int32, (16, codes), 0)
    for g in range(group):
        book = book_ref[g]
        scaled = book.astype(jnp.bfloat16).astype(jnp.float32) * (0.5 * LOG2E)
        squares = jnp.sum(book * book, axis=0, keepdims=True) * (-0.25 * LOG2E)
        one, two, three = (s.astype(jnp.float32) for s in split_three(squares))
        bias = jnp.where(row == 0, one, jnp.where(row == 1, two, jnp.where(row == 2, three, 0.0)))
        lhs = jnp.concatenate([*split_three(scaled), bias.astype(jnp.bfloat16)], axis=0)
        feat = feat_ref[g]
        rhs = jnp.concatenate([feat, feat, feat, ones], axis=0)
        feat_one = jnp.concatenate([feat, ones], axis=0)
        stats = None
        for start in range(0, rows, chunk):
            logits = lax.dot_general(
                lhs, rhs[:, start : start + chunk], (((0,), (0,)), ((), ())),
                preferred_element_type=jnp.float32,
            )
            exponent = jnp.exp2(logits - jnp.max(logits, axis=0, keepdims=True))
            inverse = 1.0 / jnp.sum(exponent, axis=0, keepdims=True)
            weights = (exponent * inverse).astype(jnp.bfloat16)
            for ref in weights_refs:
                ref[g, :, start : start + chunk] = weights
            part = lax.dot_general(
                feat_one[:, start : start + chunk], weights, (((1,), (1,)), ((), ())),
                preferred_element_type=jnp.float32,
            )
            stats = part if stats is None else stats + part
        stats_ref[g] = stats[:STAT_ROWS]


def subspace_pass(pieces, books, keep_weights):
    subs, dim, rows = pieces.shape
    codes = books.shape[2]
    group = 4 if subs % 4 == 0 else 1
    out_shape = [jax.ShapeDtypeStruct((subs, STAT_ROWS, codes), jnp.float32)]
    out_specs = [pl.BlockSpec((group, STAT_ROWS, codes), lambda i: (i, 0, 0))]
    if keep_weights:
        out_shape.append(jax.ShapeDtypeStruct((subs, codes, rows), jnp.bfloat16))
        out_specs.append(pl.BlockSpec((group, codes, rows), lambda i: (i, 0, 0)))
    return pl.pallas_call(
        pass_kernel,
        grid=(subs // group,),
        out_shape=out_shape,
        in_specs=[
            pl.BlockSpec((group, dim, rows), lambda i: (i, 0, 0)),
            pl.BlockSpec((group, dim, codes), lambda i: (i, 0, 0)),
        ],
        out_specs=out_specs,
        compiler_params=pltpu.CompilerParams(vmem_limit_bytes=32 * 2**20),
        cost_estimate=pl.CostEstimate(
            flops=subs * codes * rows * 128,
            bytes_accessed=subs * codes * rows * 2,
            transcendentals=subs * codes * rows,
        ),
    )(pieces, books)


def exchange(n, part_ref, finish, total_ref, low_ref, got_pair, low_pair, got, sems):
    pair_send, pair_recv, send, recv, out_send, out_recv, last_send, last_recv = sems
    half = n // 2
    me = lax.axis_index("rows")
    mine, side = me // 2, lax.rem(me, 2)
    sibling = me + 1 - 2 * side

    barrier = pltpu.get_barrier_semaphore()
    pl.semaphore_signal(barrier, inc=1, device_id={"rows": sibling}, device_id_type=MESH)
    for d in range(1, half):
        peer = lax.rem(mine + d, half) * 2 + side
        pl.semaphore_signal(barrier, inc=1, device_id={"rows": peer}, device_id_type=MESH)
    pl.semaphore_wait(barrier, half)

    pair = pltpu.make_async_remote_copy(
        src_ref=part_ref.at[:, 1 - side], dst_ref=got_pair, send_sem=pair_send, recv_sem=pair_recv,
        device_id={"rows": sibling}, device_id_type=MESH,
    )
    pair.start()
    pair.wait()

    copies = []
    for d in range(1, half):
        spot = lax.rem(mine + d, half)
        summed = part_ref[spot, side].astype(jnp.float32) + got_pair[spot].astype(jnp.float32)
        low_pair[spot] = summed.astype(low_pair.dtype)
        copy = pltpu.make_async_remote_copy(
            src_ref=low_pair.at[spot], dst_ref=got.at[d], send_sem=send.at[d], recv_sem=recv.at[d],
            device_id={"rows": spot * 2 + side}, device_id_type=MESH,
        )
        copy.start()
        copies.append(copy)
    total = part_ref[mine, side].astype(jnp.float32) + got_pair[mine].astype(jnp.float32)
    for d in range(1, half):
        copies[d - 1].wait_recv()
        total += got[d].astype(jnp.float32)
    result = finish(total)
    if total_ref is not None:
        total_ref[...] = result
    low_ref[mine, side] = result.astype(low_ref.dtype)

    outs = []
    for d in range(1, half):
        spot = lax.rem(mine + d, half)
        copy = pltpu.make_async_remote_copy(
            src_ref=low_ref.at[mine, side], dst_ref=low_ref.at[mine, side],
            send_sem=out_send.at[d], recv_sem=out_recv.at[d],
            device_id={"rows": spot * 2 + side}, device_id_type=MESH,
        )
        copy.start()
        outs.append(copy)
    for copy in copies:
        copy.wait_send()
    for copy in outs:
        copy.wait()
    last = pltpu.make_async_remote_copy(
        src_ref=low_ref.at[:, side], dst_ref=low_ref.at[:, side],
        send_sem=last_send, recv_sem=last_recv, device_id={"rows": sibling}, device_id_type=MESH,
    )
    last.start()
    last.wait()


def books_kernel(n, part_ref, old_ref, new_ref, got_pair, low_pair, got, *sems):
    me = lax.axis_index("rows")
    old = old_ref[me // 2, lax.rem(me, 2)]

    def finish(total):
        top = total[:, :SUB_DIM] + prior_weight * old
        return top / (total[:, SUB_DIM : SUB_DIM + 1] + prior_weight)

    exchange(n, part_ref, finish, None, new_ref, got_pair, low_pair, got, sems)


def cross_kernel(n, part_ref, total_ref, low_ref, got_pair, low_pair, got, *sems):
    exchange(n, part_ref, lambda total: total, total_ref, low_ref, got_pair, low_pair, got, sems)


def scratch(n, piece, dtype):
    half = n // 2
    one, many = pltpu.SemaphoreType.DMA, pltpu.SemaphoreType.DMA((half,))
    return [pltpu.VMEM((half, *piece), dtype)] * 3 + [one, one, many, many, many, many, one, one]


def whole_in_vmem(count):
    return [pl.BlockSpec(memory_space=pltpu.VMEM)] * count


def update_books(n, stats, books, collective_id):
    subs, dim, codes = books.shape
    if n % 2 or subs % n:
        stats = lax.psum(stats, "rows")
        top = stats[:, :SUB_DIM] + prior_weight * books
        return top / (stats[:, SUB_DIM : SUB_DIM + 1] + prior_weight)
    own = subs // n
    return pl.pallas_call(
        functools.partial(books_kernel, n),
        out_shape=jax.ShapeDtypeStruct((n // 2, 2, own, dim, codes), jnp.float32),
        in_specs=whole_in_vmem(2),
        out_specs=whole_in_vmem(1)[0],
        scratch_shapes=scratch(n, (own, STAT_ROWS, codes), jnp.float32),
        compiler_params=pltpu.CompilerParams(
            collective_id=collective_id, has_side_effects=True, vmem_limit_bytes=32 * 2**20
        ),
    )(
        stats.reshape(n // 2, 2, own, STAT_ROWS, codes), books.reshape(n // 2, 2, own, dim, codes)
    ).reshape(books.shape)


def sum_cross(n, partial, collective_id):
    height, width = partial.shape
    own = height // n
    total, low = pl.pallas_call(
        functools.partial(cross_kernel, n),
        out_shape=[
            jax.ShapeDtypeStruct((own, width), jnp.float32),
            jax.ShapeDtypeStruct((n // 2, 2, own, width), jnp.bfloat16),
        ],
        in_specs=whole_in_vmem(1),
        out_specs=whole_in_vmem(2),
        scratch_shapes=scratch(n, (own, width), jnp.bfloat16),
        compiler_params=pltpu.CompilerParams(
            collective_id=collective_id, has_side_effects=True, vmem_limit_bytes=32 * 2**20
        ),
    )(partial.reshape(n // 2, 2, own, width))
    return total, low.reshape(height, width)


def product(a, b, b_side=0):
    return lax.dot_general(
        a.astype(jnp.bfloat16), b, (((1,), (b_side,)), ((), ())), preferred_element_type=jnp.float32
    )


def per_device(n, n_sub, embeddings, rotation, codebooks):
    def over_sub(value):
        return lax.psum(value, "sub") if n_sub > 1 else value

    row_count = embeddings.shape[0]
    width = rotation.shape[1]
    subs = codebooks.shape[0]
    full_x = embeddings
    if n_sub > 1:
        full_x = lax.all_gather(embeddings, "sub", axis=1, tiled=True)
    rotated = lax.dot_general(
        rotation, full_x, (((0,), (1,)), ((), ())), preferred_element_type=jnp.float32
    ).astype(jnp.bfloat16)
    pieces = rotated.reshape(subs, SUB_DIM, row_count)
    books = codebooks
    for repeat in range(ITERS):
        stats, *weights = subspace_pass(pieces, books, repeat == ITERS - 1)
        books = update_books(n, stats, books, repeat)
    rebuilt = jnp.einsum(
        "mdk,mkr->mdr", books.astype(jnp.bfloat16), weights[0], preferred_element_type=jnp.float32
    )
    rebuilt = rebuilt.reshape(width, row_count).astype(jnp.bfloat16)
    partial = lax.dot_general(
        full_x, rebuilt, (((0,), (1,)), ((), ())), preferred_element_type=jnp.float32
    ).astype(jnp.bfloat16)
    own, low = sum_cross(n, partial, ITERS)

    wide = low.astype(jnp.float32)
    inverse = lax.rsqrt(over_sub(jnp.sum(wide * wide)) + 1e-06)
    gram = (over_sub(product(low, low, 1)) * (inverse * inverse)).astype(jnp.bfloat16)
    image = product(gram, low) * inverse
    second = product(gram, image.astype(jnp.bfloat16))
    change = quintic_three * image + quintic_five * second
    polar = (quintic_one * inverse * wide + change).astype(jnp.bfloat16)
    own_height = own.shape[0]
    own_change = lax.dynamic_slice_in_dim(change, lax.axis_index("rows") * own_height, own_height, 0)
    own = quintic_one * inverse * own + own_change

    gram_rows = over_sub(product(own, polar, 1))
    image_rows = product(gram_rows, polar)
    second_rows = product(over_sub(product(image_rows, polar, 1)), polar)
    own = quintic_one * own + quintic_three * image_rows + quintic_five * second_rows
    return (books, own)


def solution(mesh):
    return jax.shard_map(
        functools.partial(per_device, mesh.shape["rows"], mesh.shape["sub"]),
        mesh=mesh,
        in_specs=(P("rows", "sub"), P(None, "sub"), P("sub", None, None)),
        out_specs=(P("sub", None, None), P("rows", "sub")),
        check_vma=False,
    )
```

profile of v0, /device:TPU:29, one launch (start us, length us, event | category | flops | bytes accessed | tf_op | source)
XLA Modules:
  0.0 227.8 jit_solution(10238343086780968140)
XLA Ops:
  0.6 0.0 copy-start
  0.6 1.6 copy-done
  2.2 0.0 copy-start.3
  2.2 2.6 %convolution_convert_fusion.1 = bf16[1024,512]{1,0:T(8,128)(2,1)S(1)} fusion(bf16[1024,1024]{1,0:T(8,128)(2,1)S(1)} %copy-done, bf16[512,1024]{1,0:T(8,128)(2,1)} %param.3), kind=kOutput, calls=%fused_computation.7 | convolution fusion | flops 1074266112 | bytes 4194304 | tf_op jit(solution)/shard_map/dot_general | solution.py:236
  4.8 0.0 copy-done.3
  4.9 21.3 %shard_map.50 = f32[64,24,256]{2,1,0:T(8,128)S(1)} custom-call(bf16[64,16,512]{2,1,0:T(8,128)(2,1)S(1)} %bitcast.35, f32[64,16,256]{2,1,0:T(8,128)S(1)} %copy-done.3), custom_call_target="tpu_custom_call" | custom-call | flops 1073741824 | bytes 16777216 | tf_op jit(solution)/shard_map/pallas_call | solution.py:74
  26.1 40.9 %shard_map.51.old_ref = f32[16,2,2,16,256]{4,3,2,1,0:T(8,128)S(1)} custom-call(f32[16,2,2,24,256]{4,3,2,1,0:T(8,128)S(1)} %bitcast.33, f32[16,2,2,16,256]{4,3,2,1,0:T(8,128)S(1)} %bitcast.34), custom_call_target="tpu_custom_call" | custom-call | tf_op jit(solution)/shard_map/pallas_call | solution.py:187
  67.1 21.8 %shard_map.52 = (f32[64,24,256]{2,1,0:T(8,128)S(1)}, bf16[64,256,512]{2,1,0:T(8,128)(2,1)S(1)}) custom-call(bf16[64,16,512]{2,1,0:T(8,128)(2,1)S(1)} %bitcast.36, f32[64,16,256]{2,1,0:T(8,128)S(1)} %bitcast.28), custom_call_target="tpu_custom_call" | custom-call | flops 1073741824 | bytes 16777216 | tf_op jit(solution)/shard_map/pallas_call | solution.py:74
  88.9 42.0 %shard_map.53 = f32[16,2,2,16,256]{4,3,2,1,0:T(8,128)S(1)} custom-call(f32[16,2,2,24,256]{4,3,2,1,0:T(8,128)S(1)} %bitcast.32, f32[16,2,2,16,256]{4,3,2,1,0:T(8,128)S(1)} %shard_map.51.old_ref), custom_call_target="tpu_custom_call" | custom-call | tf_op jit(solution)/shard_map/pallas_call | solution.py:187
  130.8 0.0 copy-start.4
  130.8 2.3 %convolution_convert_fusion.2 = bf16[64,16,512]{2,1,0:T(8,128)(2,1)S(1)} fusion(bf16[64,256,512]{2,1,0:T(8,128)(2,1)S(1)} %get-tuple-element.7, f32[64,16,256]{2,1,0:T(8,128)S(1)} %bitcast.26), kind=kOutput, calls=%fused_computation.8 | convolution fusion | flops 269221888 | bytes 18874368 | tf_op jit(solution)/shard_map/mdk,mkr->mdr/dot_general | solution.py:244
  133.1 0.0 copy-done.4
  133.1 1.3 convolution_convert_fusion
  134.5 60.9 %shard_map.54 = (f32[32,1024]{1,0:T(8,128)S(1)}, bf16[16,2,32,1024]{3,2,1,0:T(8,128)(2,1)S(1)}) custom-call(bf16[16,2,32,1024]{3,2,1,0:T(8,128)(2,1)S(1)} %bitcast.31), custom_call_target="tpu_custom_call" | custom-call | tf_op jit(solution)/shard_map/pallas_call | solution.py:204
  195.4 0.0 copy-start.1
  195.4 1.3 copy-done.1
  196.7 1.7 multiply_reduce_fusion
  199.1 0.0 copy-start.2
  199.1 4.7 %multiply_convert_fusion = bf16[1024,1024]{1,0:T(8,128)(2,1)S(1)} fusion(bf16[1024,1024]{1,0:T(8,128)(2,1)} %bitcast.29, f32[]{:T(128)S(6)} %mul.72), kind=kOutput, calls=%fused_computation.2 | convolution fusion | flops 2149580800 | bytes 4194308 | tf_op jit(solution)/shard_map/dot_general | solution.py:221
  203.9 0.0 copy-start.5
  203.9 1.3 copy-done.5
  205.2 0.0 copy-done.2
  205.2 4.3 %fusion.10 = f32[1024,1024]{1,0:T(8,128)} fusion(bf16[1024,1024]{1,0:T(8,128)(2,1)S(1)} %multiply_convert_fusion, bf16[1024,1024]{1,0:T(8,128)(2,1)S(1)} %bitcast.30), kind=kOutput, calls=%fused_computation.19 | convolution fusion | flops 2147483648 | bytes 8388608 | tf_op jit(solution)/shard_map/dot_general | solution.py:221
  209.5 10.0 %add_convert_fusion = (bf16[1024,1024]{1,0:T(8,128)(2,1)}, f32[1024,1024]{1,0:T(8,128)}) fusion(f32[]{:T(128)S(6)} %mul.69, bf16[16,2,32,1024]{3,2,1,0:T(8,128)(2,1)} %copy-done.1, bf16[1024,1024]{1,0:T(8,128)(2,1)} %copy-done.5, f32[1024,1024]{1,0:T(8,128)} %fusion.10, f32[]{:T(128)S(6)} %rsqrt.3), kind=kOutput, calls=%fused_computation | convolution fusion | flops 2157969408 | bytes 14680072 | tf_op jit(solution)/shard_map/dot_general | solution.py:221
  219.5 3.4 %fusion.2 = f32[32,1024]{1,0:T(8,128)S(1)} fusion(bf16[1024,1024]{1,0:T(8,128)(2,1)} %get-tuple-element.10, f32[1024,1024]{1,0:T(8,128)} %get-tuple-element.11, s32[]{:T(128)S(6)} %select_n.3, f32[32,1024]{1,0:T(8,128)S(1)} %get-tuple-element.9, f32[]{:T(128)S(6)} %mul.69), kind=kOutput, calls=%fused_computation.13 | convolution fusion | flops 134348800 | bytes 4587528 | tf_op jit(solution)/shard_map/dot_general | solution.py:221
  222.8 4.0 %fusion.1 = f32[32,1024]{1,0:T(8,128)} fusion(bf16[1024,1024]{1,0:T(8,128)(2,1)} %get-tuple-element.10, f32[32,1024]{1,0:T(8,128)S(1)} %fusion.2, f32[1024,1024]{1,0:T(8,128)} %get-tuple-element.11, s32[]{:T(128)S(6)} %select_n.3, f32[32,1024]{1,0:T(8,128)S(1)} %get-tuple-element.9, f32[]{:T(128)S(6)} %mul.69), kind=kOutput, calls=%fused_computation.10 | convolution fusion | flops 134512640 | bytes 4849672 | tf_op jit(solution)/shard_map/dot_general | solution.py:221
  226.9 1.0 copy.6
Async XLA Ops:
  0.6 1.6 copy-start
  2.2 2.6 %copy-start.3 = (f32[64,16,256]{2,1,0:T(8,128)S(1)}, f32[64,16,256]{2,1,0:T(8,128)}, u32[]{:S(2)}) copy-start(f32[64,16,256]{2,1,0:T(8,128)} %book_ref.1) | copy-start | bytes 3145732
  130.8 2.3 %copy-start.4 = (bf16[512,1024]{1,0:T(8,128)(2,1)S(1)}, bf16[512,1024]{1,0:T(8,128)(2,1)}, u32[]{:S(2)}) copy-start(bf16[512,1024]{1,0:T(8,128)(2,1)} %param.3) | copy-start | bytes 3145732
  195.4 1.4 copy-start.1
  199.1 6.1 %copy-start.2 = (bf16[16,2,32,1024]{3,2,1,0:T(8,128)(2,1)S(1)}, bf16[16,2,32,1024]{3,2,1,0:T(8,128)(2,1)}, u32[]{:S(2)}) copy-start(bf16[16,2,32,1024]{3,2,1,0:T(8,128)(2,1)} %copy-done.1) | copy-start | bytes 6291460
  203.9 1.3 copy-start.5
where the time goes:
time: 228 us
  Pallas kernels  187 us (82%)
  matrix products  32.6 us (14%)
  local copies, waits for them, and re-layouts  5.25 us (2%)
    pallas_call x2, Pallas kernels, update_books(): pl.pallas_call(functools.partial(books_kernel, n), out_shape=jax.ShapeDty...  82.9 us
    pallas_call x1, Pallas kernels, sum_cross(): pl.pallas_call(functools.partial(cross_kernel, n), out_shape=[jax.ShapeDt...  60.9 us
    pallas_call x2, Pallas kernels, subspace_pass(): pl.pallas_call(pass_kernel, grid=(subs // group,), out_shape=out_shape, i...  43.1 us
    dot_general x5, matrix products, product(): lax.dot_general(a.astype(jnp.bfloat16), b, (((1,), (b_side,)), ((), ())),...  26.4 us
    unnamed x13, local copies, waits for them, and re-layouts  5.25 us

commit v1 on v0

--- a/solution.py
+++ b/solution.py
@@ -10,7 +10,6 @@
 SUB_DIM = 16
 ITERS = 2
 LOG2E = 1.4426950408889634
-STAT_ROWS = 24
 
 prior_weight = 8.0
 quintic_one = 3.4445
@@ -27,18 +26,22 @@
     return high, middle, low
 
 
-def pass_kernel(feat_ref, book_ref, stats_ref, *weights_refs):
+def pass_kernel(own, packed, feat_ref, book_ref, stats_ref, *weights_refs):
     group, dim, rows = feat_ref.shape
     codes = book_ref.shape[2]
     chunk = 256 if rows % 256 == 0 else rows
     ones = jnp.ones((16, rows), jnp.bfloat16)
     row = lax.broadcasted_iota(jnp.int32, (16, codes), 0)
     for g in range(group):
-        book = book_ref[g]
-        scaled = book.astype(jnp.bfloat16).astype(jnp.float32) * (0.5 * LOG2E)
-        squares = jnp.sum(book * book, axis=0, keepdims=True) * (-0.25 * LOG2E)
-        one, two, three = (s.astype(jnp.float32) for s in split_three(squares))
-        bias = jnp.where(row == 0, one, jnp.where(row == 1, two, jnp.where(row == 2, three, 0.0)))
+        piece, spot = g // own, g % own
+        if packed:
+            low = book_ref[piece, spot * dim : spot * dim + dim]
+            tile = book_ref[piece, own * dim :].astype(jnp.float32)
+            bias = jnp.where((row >= 3 * spot) & (row < 3 * spot + 3), tile, 0.0)
+        else:
+            low = book_ref[g].astype(jnp.bfloat16)
+            bias = square_rows(row, 0, book_ref[g], 0.0)
+        scaled = low.astype(jnp.float32) * (0.5 * LOG2E)
         lhs = jnp.concatenate([*split_three(scaled), bias.astype(jnp.bfloat16)], axis=0)
         feat = feat_ref[g]
         rhs = jnp.concatenate([feat, feat, feat, ones], axis=0)
@@ -59,25 +62,38 @@
                 preferred_element_type=jnp.float32,
             )
             stats = part if stats is None else stats + part
-        stats_ref[g] = stats[:STAT_ROWS]
-
-
-def subspace_pass(pieces, books, keep_weights):
+        stats_ref[piece, spot * dim : spot * dim + dim] = stats[:dim]
+        counts = jnp.where(row == spot, stats[dim:], 0.0 if spot == 0 else counts)
+        if spot == own - 1:
+            stats_ref[piece, own * dim :] = counts
+
+
+def square_rows(row, spot, book, others):
+    squares = jnp.sum(book * book, axis=0, keepdims=True) * (-0.25 * LOG2E)
+    for k, term in enumerate(split_three(squares)):
+        others = jnp.where(row == 3 * spot + k, term.astype(jnp.float32), others)
+    return others
+
+
+def subspace_pass(own, pieces, books, keep_weights):
     subs, dim, rows = pieces.shape
+    packed = books.dtype == jnp.bfloat16
     codes = books.shape[2]
-    group = 4 if subs % 4 == 0 else 1
-    out_shape = [jax.ShapeDtypeStruct((subs, STAT_ROWS, codes), jnp.float32)]
-    out_specs = [pl.BlockSpec((group, STAT_ROWS, codes), lambda i: (i, 0, 0))]
+    group = max(own, 4 if subs % 4 == 0 else 1)
+    height = own * dim + 16
+    out_shape = [jax.ShapeDtypeStruct((subs // own, height, codes), jnp.float32)]
+    out_specs = [pl.BlockSpec((group // own, height, codes), lambda i: (i, 0, 0))]
     if keep_weights:
         out_shape.append(jax.ShapeDtypeStruct((subs, codes, rows), jnp.bfloat16))
         out_specs.append(pl.BlockSpec((group, codes, rows), lambda i: (i, 0, 0)))
+    book_block = (group // own, height, codes) if packed else (group, dim, codes)
     return pl.pallas_call(
-        pass_kernel,
+        functools.partial(pass_kernel, own, packed),
         grid=(subs // group,),
         out_shape=out_shape,
         in_specs=[
             pl.BlockSpec((group, dim, rows), lambda i: (i, 0, 0)),
-            pl.BlockSpec((group, dim, codes), lambda i: (i, 0, 0)),
+            pl.BlockSpec(book_block, lambda i: (i, 0, 0)),
         ],
         out_specs=out_specs,
         compiler_params=pltpu.CompilerParams(vmem_limit_bytes=32 * 2**20),
@@ -89,7 +105,8 @@
     )(pieces, books)
 
 
-def exchange(n, part_ref, finish, total_ref, low_ref, got_pair, low_pair, got, sems):
+def exchange(n, part_ref, finish, total_ref, low_ref, buffers, sems):
+    got_pair, low_pair, got, *sent_pair = buffers
     pair_send, pair_recv, send, recv, out_send, out_recv, last_send, last_recv = sems
     half = n // 2
     me = lax.axis_index("rows")
@@ -101,10 +118,16 @@
     for d in range(1, half):
         peer = lax.rem(mine + d, half) * 2 + side
         pl.semaphore_signal(barrier, inc=1, device_id={"rows": peer}, device_id_type=MESH)
+    if sent_pair:
+        for spot in range(half):
+            sent_pair[0][spot] = part_ref[spot, 1 - side].astype(jnp.bfloat16)
+        pair_source = sent_pair[0]
+    else:
+        pair_source = part_ref.at[:, 1 - side]
     pl.semaphore_wait(barrier, half)
 
     pair = pltpu.make_async_remote_copy(
-        src_ref=part_ref.at[:, 1 - side], dst_ref=got_pair, send_sem=pair_send, recv_sem=pair_recv,
+        src_ref=pair_source, dst_ref=got_pair, send_sem=pair_send, recv_sem=pair_recv,
         device_id={"rows": sibling}, device_id_type=MESH,
     )
     pair.start()
@@ -125,10 +148,9 @@
     for d in range(1, half):
         copies[d - 1].wait_recv()
         total += got[d].astype(jnp.float32)
-    result = finish(total)
-    if total_ref is not None:
-        total_ref[...] = result
-    low_ref[mine, side] = result.astype(low_ref.dtype)
+    kept, shared = finish(total)
+    total_ref[...] = kept
+    low_ref[mine, side] = shared
 
     outs = []
     for d in range(1, half):
@@ -152,50 +174,60 @@
     last.wait()
 
 
-def books_kernel(n, part_ref, old_ref, new_ref, got_pair, low_pair, got, *sems):
-    me = lax.axis_index("rows")
-    old = old_ref[me // 2, lax.rem(me, 2)]
+def books_kernel(n, part_ref, old_ref, new_ref, low_ref, *rest):
+    own, dim, codes = old_ref.shape
+    row = lax.broadcasted_iota(jnp.int32, (16, codes), 0)
 
     def finish(total):
-        top = total[:, :SUB_DIM] + prior_weight * old
-        return top / (total[:, SUB_DIM : SUB_DIM + 1] + prior_weight)
-
-    exchange(n, part_ref, finish, None, new_ref, got_pair, low_pair, got, sems)
-
-
-def cross_kernel(n, part_ref, total_ref, low_ref, got_pair, low_pair, got, *sems):
-    exchange(n, part_ref, lambda total: total, total_ref, low_ref, got_pair, low_pair, got, sems)
-
-
-def scratch(n, piece, dtype):
+        kept, bias = [], 0.0
+        for spot in range(own):
+            top = total[spot * dim : spot * dim + dim] + prior_weight * old_ref[spot]
+            count = total[own * dim + spot : own * dim + spot + 1]
+            kept.append(top / (count + prior_weight))
+            bias = square_rows(row, spot, kept[spot], bias)
+        shared = kept if low_ref.shape[2] == own * dim else kept + [bias]
+        low = jnp.concatenate([part.astype(jnp.bfloat16) for part in shared], axis=0)
+        return jnp.stack(kept), low
+
+    exchange(n, part_ref, finish, new_ref, low_ref, rest[:4], rest[4:])
+
+
+def cross_kernel(n, part_ref, total_ref, low_ref, *rest):
+    def finish(total):
+        return total, total.astype(jnp.bfloat16)
+
+    exchange(n, part_ref, finish, total_ref, low_ref, rest[:3], rest[3:])
+
+
+def scratch(n, piece, buffers):
     half = n // 2
     one, many = pltpu.SemaphoreType.DMA, pltpu.SemaphoreType.DMA((half,))
-    return [pltpu.VMEM((half, *piece), dtype)] * 3 + [one, one, many, many, many, many, one, one]
+    slots = [pltpu.VMEM((half, *piece), jnp.bfloat16)] * buffers
+    return slots + [one, one, many, many, many, many, one, one]
 
 
 def whole_in_vmem(count):
     return [pl.BlockSpec(memory_space=pltpu.VMEM)] * count
 
 
-def update_books(n, stats, books, collective_id):
-    subs, dim, codes = books.shape
-    if n % 2 or subs % n:
-        stats = lax.psum(stats, "rows")
-        top = stats[:, :SUB_DIM] + prior_weight * books
-        return top / (stats[:, SUB_DIM : SUB_DIM + 1] + prior_weight)
-    own = subs // n
-    return pl.pallas_call(
+def update_books(n, stats, old, last, collective_id):
+    own, dim, codes = old.shape
+    height = stats.shape[1]
+    kept = own * dim if last else height
+    new, low = pl.pallas_call(
         functools.partial(books_kernel, n),
-        out_shape=jax.ShapeDtypeStruct((n // 2, 2, own, dim, codes), jnp.float32),
+        out_shape=[
+            jax.ShapeDtypeStruct(old.shape, jnp.float32),
+            jax.ShapeDtypeStruct((n // 2, 2, kept, codes), jnp.bfloat16),
+        ],
         in_specs=whole_in_vmem(2),
-        out_specs=whole_in_vmem(1)[0],
-        scratch_shapes=scratch(n, (own, STAT_ROWS, codes), jnp.float32),
+        out_specs=whole_in_vmem(2),
+        scratch_shapes=scratch(n, (height, codes), 4),
         compiler_params=pltpu.CompilerParams(
             collective_id=collective_id, has_side_effects=True, vmem_limit_bytes=32 * 2**20
         ),
-    )(
-        stats.reshape(n // 2, 2, own, STAT_ROWS, codes), books.reshape(n // 2, 2, own, dim, codes)
-    ).reshape(books.shape)
+    )(stats.reshape(n // 2, 2, height, codes), old)
+    return new, low.reshape(n, kept, codes)
 
 
 def sum_cross(n, partial, collective_id):
@@ -209,7 +241,7 @@
         ],
         in_specs=whole_in_vmem(1),
         out_specs=whole_in_vmem(2),
-        scratch_shapes=scratch(n, (own, width), jnp.bfloat16),
+        scratch_shapes=scratch(n, (own, width), 3),
         compiler_params=pltpu.CompilerParams(
             collective_id=collective_id, has_side_effects=True, vmem_limit_bytes=32 * 2**20
         ),
@@ -217,9 +249,67 @@
     return total, low.reshape(height, width)
 
 
+def polar_kernel(own_ref, low_ref, out_ref, gram_ref, image_ref, change_ref, polar_ref):
+    size = low_ref.shape[0]
+    own_height = own_ref.shape[0]
+    tile = 256 if size % 256 == 0 else size
+    tiles = size // tile
+
+    def rows(i):
+        return pl.ds(pl.multiple_of(i * tile, tile), tile)
+
+    def square(i, total):
+        wide = low_ref[rows(i)].astype(jnp.float32)
+        return total + jnp.sum(wide * wide, axis=0, keepdims=True)
+
+    squares = lax.fori_loop(0, tiles, square, jnp.zeros((1, low_ref.shape[1]), jnp.float32))
+    inverse = lax.rsqrt(jnp.sum(squares, axis=1, keepdims=True) + 1e-06)
+
+    @pl.loop(0, tiles)
+    def _(i):
+        gram = product(low_ref[rows(i)], low_ref[...], 1) * (inverse * inverse)
+        gram_ref[rows(i)] = gram.astype(jnp.bfloat16)
+
+    @pl.loop(0, tiles)
+    def _(i):
+        image = product(gram_ref[rows(i)], low_ref[...]) * inverse
+        image_ref[rows(i)] = image.astype(jnp.bfloat16)
+        change_ref[rows(i)] = quintic_three * image
+
+    @pl.loop(0, tiles)
+    def _(i):
+        change = change_ref[rows(i)] + quintic_five * product(gram_ref[rows(i)], image_ref[...])
+        change_ref[rows(i)] = change
+        polar = quintic_one * inverse * low_ref[rows(i)].astype(jnp.float32) + change
+        polar_ref[rows(i)] = polar.astype(jnp.bfloat16)
+
+    start = pl.multiple_of(lax.axis_index("rows") * own_height, own_height)
+    own = quintic_one * inverse * own_ref[...] + change_ref[pl.ds(start, own_height)]
+    image = product(product(own, polar_ref[...], 1), polar_ref[...])
+    second = product(product(image, polar_ref[...], 1), polar_ref[...])
+    out_ref[...] = quintic_one * own + quintic_three * image + quintic_five * second
+
+
+def polar_steps(own, low):
+    size, width = low.shape
+    return pl.pallas_call(
+        polar_kernel,
+        out_shape=jax.ShapeDtypeStruct(own.shape, jnp.float32),
+        in_specs=whole_in_vmem(2),
+        out_specs=whole_in_vmem(1)[0],
+        scratch_shapes=[
+            pltpu.VMEM((size, size), jnp.bfloat16),
+            pltpu.VMEM((size, width), jnp.bfloat16),
+            pltpu.VMEM((size, width), jnp.float32),
+            pltpu.VMEM((size, width), jnp.bfloat16),
+        ],
+        compiler_params=pltpu.CompilerParams(vmem_limit_bytes=40 * 2**20),
+    )(own, low)
+
+
 def product(a, b, b_side=0):
     return lax.dot_general(
-        a.astype(jnp.bfloat16), b, (((1,), (b_side,)), ((), ())), preferred_element_type=jnp.float32
+        a.astype(jnp.bfloat16), b.astype(jnp.bfloat16), (((1,), (b_side,)), ((), ())), preferred_element_type=jnp.float32
     )
 
 
@@ -237,18 +327,32 @@
         rotation, full_x, (((0,), (1,)), ((), ())), preferred_element_type=jnp.float32
     ).astype(jnp.bfloat16)
     pieces = rotated.reshape(subs, SUB_DIM, row_count)
-    books = codebooks
+    split_books = n % 2 == 0 and subs % n == 0 and 3 * (subs // n) <= 16
+    own_subs = subs // n if split_books else 1
+    books, own = codebooks, codebooks
+    if split_books:
+        own = lax.dynamic_slice_in_dim(codebooks, lax.axis_index("rows") * own_subs, own_subs, 0)
     for repeat in range(ITERS):
-        stats, *weights = subspace_pass(pieces, books, repeat == ITERS - 1)
-        books = update_books(n, stats, books, repeat)
+        last = repeat == ITERS - 1
+        stats, *weights = subspace_pass(own_subs, pieces, books, last)
+        if split_books:
+            own, books = update_books(n, stats, own, last, repeat)
+        else:
+            stats = lax.psum(stats, "rows")
+            top = stats[:, :SUB_DIM] + prior_weight * books
+            books = top / (stats[:, SUB_DIM : SUB_DIM + 1] + prior_weight)
+    books = books.reshape(codebooks.shape)
     rebuilt = jnp.einsum(
         "mdk,mkr->mdr", books.astype(jnp.bfloat16), weights[0], preferred_element_type=jnp.float32
     )
+    books = books.astype(jnp.float32)
     rebuilt = rebuilt.reshape(width, row_count).astype(jnp.bfloat16)
     partial = lax.dot_general(
         full_x, rebuilt, (((0,), (1,)), ((), ())), preferred_element_type=jnp.float32
     ).astype(jnp.bfloat16)
     own, low = sum_cross(n, partial, ITERS)
+    if n_sub == 1:
+        return (books, polar_steps(own, low))
 
     wide = low.astype(jnp.float32)
     inverse = lax.rsqrt(over_sub(jnp.sum(wide * wide)) + 1e-06)

time: 228 us -> 178 us (0.78)
  matrix products: 32.6 us -> 6.18 us
  Pallas kernels: 187 us -> 168 us
  local copies, waits for them, and re-layouts: 5.25 us -> 1.61 us
    dot_general x5 -> x0, matrix products: 26.4 us -> none  [product(): lax.dot_general(a.astype(jnp.bfloat16), b, (((1,), (b_side,)), ((), ())),...]
    pallas_call x4 -> x5, Pallas kernels: 126 us -> 109 us  [the longest x2 54.3 us: update_books(): pl.pallas_call(functools.partial(books_kernel, n), out_shape=[jax.ShapeDt...]
    unnamed x13 -> x6, local copies, waits for them, and re-layouts: 5.25 us -> 0.7 us
where the time goes in v1:
time: 178 us
  Pallas kernels  168 us (94%)
  matrix products  6.18 us (3%)
    pallas_call x1, Pallas kernels, sum_cross(): pl.pallas_call(functools.partial(cross_kernel, n), out_shape=[jax.ShapeDt...  59.4 us
    pallas_call x2, Pallas kernels, update_books(): pl.pallas_call(functools.partial(books_kernel, n), out_shape=[jax.ShapeDt...  54.3 us
    pallas_call x2, Pallas kernels, subspace_pass(): pl.pallas_call(functools.partial(pass_kernel, own, packed), grid=(subs //...  42.7 us
    pallas_call x1, Pallas kernels, polar_steps(): pl.pallas_call(polar_kernel, out_shape=jax.ShapeDtypeStruct(own.shape, jn...  11.8 us

profile of v1, /device:TPU:29, one launch (start us, length us, event | category | flops | bytes accessed | tf_op | source)
XLA Modules:
  0.0 177.9 jit_solution(9454645331627551189)
XLA Ops:
  0.6 0.0 copy-start
  0.6 0.9 constant_dynamic-slice_fusion.old_ref
  1.6 0.7 copy-done
  2.2 0.0 copy-start.1
  2.2 2.6 %convolution_convert_fusion.1 = bf16[1024,512]{1,0:T(8,128)(2,1)S(1)} fusion(bf16[1024,1024]{1,0:T(8,128)(2,1)S(1)} %copy-done, bf16[512,1024]{1,0:T(8,128)(2,1)} %param.3), kind=kOutput, calls=%fused_computation.1 | convolution fusion | flops 1074266112 | bytes 4194304 | tf_op jit(solution)/shard_map/dot_general | solution.py:326
  4.9 0.0 copy-done.1
  4.9 21.1 %shard_map.50 = f32[32,48,256]{2,1,0:T(8,128)S(1)} custom-call(bf16[64,16,512]{2,1,0:T(8,128)(2,1)S(1)} %bitcast.23, f32[64,16,256]{2,1,0:T(8,128)S(1)} %copy-done.1), custom_call_target="tpu_custom_call" | custom-call | flops 1073741824 | bytes 16777216 | tf_op jit(solution)/shard_map/pallas_call | solution.py:90
  26.0 29.1 %shard_map.51 = (f32[2,16,256]{2,1,0:T(8,128)S(1)}, bf16[16,2,48,256]{3,2,1,0:T(8,128)(2,1)S(1)}) custom-call(f32[16,2,48,256]{3,2,1,0:T(8,128)S(1)} %bitcast.21, f32[2,16,256]{2,1,0:T(8,128)S(1)} %constant_dynamic-slice_fusion.old_ref), custom_call_target="tpu_custom_call" | custom-call | tf_op jit(solution)/shard_map/pallas_call | solution.py:217
  55.2 21.5 %shard_map.52 = (f32[32,48,256]{2,1,0:T(8,128)S(1)}, bf16[64,256,512]{2,1,0:T(8,128)(2,1)S(1)}) custom-call(bf16[64,16,512]{2,1,0:T(8,128)(2,1)S(1)} %bitcast.24, bf16[32,48,256]{2,1,0:T(8,128)(2,1)S(1)} %bitcast.22), custom_call_target="tpu_custom_call" | custom-call | flops 1073741824 | bytes 16777216 | tf_op jit(solution)/shard_map/pallas_call | solution.py:90
  76.7 25.2 %shard_map.53 = (f32[2,16,256]{2,1,0:T(8,128)}, bf16[16,2,32,256]{3,2,1,0:T(8,128)(2,1)S(1)}) custom-call(f32[16,2,48,256]{3,2,1,0:T(8,128)S(1)} %bitcast.20, f32[2,16,256]{2,1,0:T(8,128)S(1)} %get-tuple-element.11.old_ref), custom_call_target="tpu_custom_call" | custom-call | tf_op jit(solution)/shard_map/pallas_call | solution.py:217
  101.9 0.0 copy-start.2
  101.9 2.3 %convolution_convert_fusion.2 = bf16[64,16,512]{2,1,0:T(8,128)(2,1)S(1)} fusion(bf16[64,16,256]{2,1,0:T(8,128)(2,1)S(1)} %bitcast.16, bf16[64,256,512]{2,1,0:T(8,128)(2,1)S(1)} %get-tuple-element.13), kind=kOutput, calls=%fused_computation.2 | convolution fusion | flops 268959744 | bytes 18350080 | tf_op jit(solution)/shard_map/mdk,mkr->mdr/dot_general | solution.py:345
  104.2 1.1 convert_element_type.19
  105.3 0.0 copy-done.2
  105.3 1.3 convolution_convert_fusion
  106.6 59.4 %shard_map.54 = (f32[32,1024]{1,0:T(8,128)S(1)}, bf16[16,2,32,1024]{3,2,1,0:T(8,128)(2,1)S(1)}) custom-call(bf16[16,2,32,1024]{3,2,1,0:T(8,128)(2,1)S(1)} %bitcast.19), custom_call_target="tpu_custom_call" | custom-call | tf_op jit(solution)/shard_map/pallas_call | solution.py:236
  166.1 11.8 %shard_map.55 = f32[32,1024]{1,0:T(8,128)} custom-call(f32[32,1024]{1,0:T(8,128)S(1)} %get-tuple-element.14.own_ref, bf16[1024,1024]{1,0:T(8,128)(2,1)S(1)} %bitcast.18), custom_call_target="tpu_custom_call" | custom-call | tf_op jit(solution)/shard_map/pallas_call | solution.py:295
Async XLA Ops:
  0.6 1.6 copy-start
  2.2 2.6 %copy-start.1 = (f32[64,16,256]{2,1,0:T(8,128)S(1)}, f32[64,16,256]{2,1,0:T(8,128)}, u32[]{:S(2)}) copy-start(f32[64,16,256]{2,1,0:T(8,128)} %book_ref.1) | copy-start | bytes 3145732
  101.9 3.4 %copy-start.2 = (bf16[512,1024]{1,0:T(8,128)(2,1)S(1)}, bf16[512,1024]{1,0:T(8,128)(2,1)}, u32[]{:S(2)}) copy-start(bf16[512,1024]{1,0:T(8,128)(2,1)} %param.3) | copy-start | bytes 3145732
